TPU v7x, 256 devices: a whole 4x4x8 slice. The times are simulated.
256 devices in a mesh: blk: 8 (over z), col: 8 (over x, y_lo), rep: 4 (over y_hi, core).
Axes of the slice: x: 4, y: 4 (y_hi: 2, y_lo: 2; y = y_hi * 2 + y_lo), z: 8, core: 2. Of those that a mesh axis runs over, the one named last changes fastest.
Arguments:
- tokens: bfloat16 [4096, 18432], P(('blk', 'rep'), 'col'), may hold values from -6 to 6
- grad_out: bfloat16 [4096, 18432], P(('blk', 'rep'), 'col'), may hold values from -6 to 6
- w_in: bfloat16 [18432, 4608], P('col', 'blk'), may hold values from -0.046875 to 0.046875
- w_out: bfloat16 [4608, 18432], P('blk', 'col'), may hold values from -0.046875 to 0.046875
Outputs:
- grad_tokens: bfloat16 [4096, 18432], P(('blk', 'rep'), 'col')
- grad_in: bfloat16 [18432, 4608], P('col', 'blk')
- grad_outw: bfloat16 [4608, 18432], P('blk', 'col')
All inputs are finite; a program needn't handle non-finite values.
Results may differ from a plain program's by a relative error of at most 0.029.
Values may be sent and summed in bfloat16 or wider, within the bound.
A program may use at most 128 MiB of HBM per device.

v0:
```python
import math

import jax
import jax.numpy as jnp
from jax import lax
from jax.sharding import PartitionSpec as P


def gelu_tanh(value):
    return jax.nn.gelu(value, approximate=True)


def activate(preact, grad_hidden):
    active, pull = jax.vjp(gelu_tanh, preact)
    return (active.astype(jnp.bfloat16), pull(grad_hidden)[0].astype(jnp.bfloat16))


def shards(tokens, grad_out, w_in, w_out):
    hid = w_in.shape[1]
    stacked = jnp.stack([tokens, grad_out])
    gathered = lax.all_gather(stacked, "blk", axis=1, tiled=True)
    pre_part = jnp.dot(gathered[0], w_in, preferred_element_type=jnp.float32)
    hid_part = jnp.einsum("td,fd->tf", gathered[1], w_out, preferred_element_type=jnp.float32)
    partial_sums = jnp.concatenate([pre_part, hid_part], axis=1)
    summed = lax.psum(partial_sums.astype(jnp.bfloat16), "col").astype(jnp.float32)
    hidden, grad_pre = activate(summed[:, :hid], summed[:, hid:])
    grad_tokens = lax.psum_scatter(
        jnp.einsum("tf,df->td", grad_pre, w_in, preferred_element_type=jnp.float32).astype(
            jnp.bfloat16
        ),
        "blk",
        scatter_dimension=0,
        tiled=True,
    )
    acc_in = jnp.einsum("td,tf->df", gathered[0], grad_pre, preferred_element_type=jnp.float32)
    acc_out = jnp.einsum("tf,td->fd", hidden, gathered[1], preferred_element_type=jnp.float32)
    total_tokens = tokens.shape[0] * lax.axis_size("blk") * lax.axis_size("rep")
    scale = 1.0 / math.sqrt(total_tokens)
    acc_in = acc_in * scale
    acc_out = acc_out * scale
    sum_in, sum_out = (
        lax.psum(acc_in.astype(jnp.bfloat16), "rep").astype(jnp.float32),
        lax.psum(acc_out.astype(jnp.bfloat16), "rep").astype(jnp.float32),
    )
    return (grad_tokens, sum_in.astype(jnp.bfloat16), sum_out.astype(jnp.bfloat16))


def solution(mesh):
    placed = (P(("blk", "rep"), "col"), P(("blk", "rep"), "col"), P("col", "blk"), P("blk", "col"))
    return jax.shard_map(
        shards,
        mesh=mesh,
        in_specs=placed,
        out_specs=(P(("blk", "rep"), "col"), P("col", "blk"), P("blk", "col")),
        check_vma=False,
    )
```

profile of v0, /device:TPU:1, one launch (start us, length us, event | category | flops | bytes accessed | tf_op | source)
XLA Modules:
  0.0 453.7 jit_solution(1823353463603752212)
XLA Ops:
  7.2 0.0 copy-start
  7.2 0.0 all-gather.2.cloned.1.call-start
  7.2 2.5 pad_maximum_fusion.1
  9.7 0.0 all-gather.2.cloned.1.call-update
  9.8 0.0 all-reduce.4.cloned.1.call-start
  9.8 108.3 %all-gather.2.cloned.1.call-done = bf16[2,1024,2304]{2,1,0:T(8,128)(2,1)} async-done(((bf16[2,128,2304]{2,1,0:T(8,128)(2,1)}), bf16[2,1024,2304]{2,1,0:T(8,128)(2,1)}) %all-gather.2.cloned.1.call-update) | async-done | bytes 9437200 | tf_op jit(solution)/shard_map/all_gather | solution.py:21
  118.2 6.2 %fusion.9 = bf16[1024,576]{0,1:T(8,128)(2,1)S(1)} fusion(bf16[576,2304]{1,0:T(8,128)(2,1)} %param.7, bf16[2,1024,2304]{2,1,0:T(8,128)(2,1)} %all-gather.2.cloned.1.call-done), kind=kOutput, calls=%fused_computation.18 | convolution fusion | flops 2718498816 | bytes 8552448 | tf_op jit(solution)/shard_map/td,fd->tf/dot_general | solution.py:23
  124.4 0.0 copy-done
  124.4 0.0 copy-done.3
  124.4 2.9 fusion.10
  127.4 1.6 pad_maximum_fusion
  129.0 0.0 all-reduce.4.cloned.1.call-update
  129.0 0.0 all-reduce.6.cloned.1.call-start
  129.1 116.7 %all-reduce.4.cloned.1.call-done = bf16[1024,1152]{0,1:T(8,128)(2,1)} async-done(((bf16[1024,1152]{0,1:T(8,128)(2,1)}), bf16[1024,1152]{0,1:T(8,128)(2,1)}) %all-reduce.4.cloned.1.call-update) | async-done | bytes 2359312 | tf_op jit(solution)/shard_map/psum | solution.py:25
  245.8 2.2 convert_element_type.23
  248.0 0.0 slice-start
  248.0 1.6 fusion.8
  249.6 0.0 copy-start.2
  249.6 0.0 slice-start.1
  249.6 0.0 slice-start.2
  249.6 7.4 %multiply_convert_fusion = bf16[576,2304]{1,0:T(8,128)(2,1)} fusion(bf16[2,1024,2304]{2,1,0:T(8,128)(2,1)} %all-gather.2.cloned.1.call-done, f32[1024,1152]{0,1:T(8,128)S(1)} %convert_element_type.23), kind=kOutput, calls=%fused_computation.1 | convolution fusion | flops 2725871616 | bytes 9732096 | tf_op jit(solution)/shard_map/tf,td->fd/dot_general | solution.py:36
  257.0 0.0 slice-done.1
  257.0 0.0 slice-done.2
  257.0 4.2 multiply_convert_fusion.1
  261.2 0.0 all-reduce.6.cloned.1.call-update
  261.3 0.0 reduce-scatter.2.cloned.1.call-start
  261.3 7.1 %convolution_convert_fusion = bf16[1024,2304]{1,0:T(8,128)(2,1)} fusion(bf16[1024,576]{0,1:T(8,128)(2,1)} %copy-done.2, bf16[2304,576]{0,1:T(8,128)(2,1)S(1)} %copy-done), kind=kOutput, calls=%fused_computation | convolution fusion | flops 2720268288 | bytes 8552448 | tf_op jit(solution)/shard_map/tf,df->td/dot_general | solution.py:28
  268.4 0.0 reduce-scatter.2.cloned.1.call-update
  268.4 111.2 %all-reduce.6.cloned.1.call-done = (bf16[2304,576]{0,1:T(8,128)(2,1)}, bf16[576,2304]{1,0:T(8,128)(2,1)}) async-done(((bf16[2304,576]{0,1:T(8,128)(2,1)}, bf16[576,2304]{1,0:T(8,128)(2,1)}), (bf16[2304,576]{0,1:T(8,128)(2,1)}, bf16[576,2304]{1,0:T(8,128)(2,1)})) %all-reduce.6.cloned.1.call-update) | async-done | bytes 5308432 | tf_op jit(solution)/shard_map/psum | solution.py:42
  379.6 62.5 %reduce-scatter.2.cloned.1.call-done = bf16[128,2304]{1,0:T(8,128)(2,1)} async-done(((bf16[1024,2304]{1,0:T(8,128)(2,1)}), bf16[128,2304]{1,0:T(8,128)(2,1)}) %reduce-scatter.2.cloned.1.call-update) | async-done | bytes 589840 | tf_op jit(solution)/shard_map/reduce_scatter | solution.py:27
  442.1 3.6 copy.10
  445.7 1.5 copy.11
  (6 shorter events, 0.0 us)
Async XLA Ops:
  7.2 117.2 %copy-start = (bf16[2304,576]{0,1:T(8,128)(2,1)S(1)}, bf16[2304,576]{0,1:T(8,128)(2,1)}, u32[]{:S(2)}) copy-start(bf16[2304,576]{0,1:T(8,128)(2,1)} %param.6) | copy-start | bytes 7962628
  7.2 111.0 %all-gather.2.cloned.1.call-start = ((), (), s32[]{:S(2)}) async-start(), calls=%async_computation.1 | async-start | bytes 10616832 | tf_op jit(solution)/shard_map/all_gather | solution.py:21
  9.8 236.0 %all-reduce.4.cloned.1.call-start = ((), (), s32[]{:S(2)}) async-start(), calls=%async_computation.2 | async-start | bytes 4718592 | tf_op jit(solution)/shard_map/psum | solution.py:25
  118.2 6.3 %copy-start.3 = (bf16[2,1024,2304]{2,1,0:T(8,128)(2,1)S(1)}, bf16[2,1024,2304]{2,1,0:T(8,128)(2,1)}, u32[]{:S(2)}) copy-start(bf16[2,1024,2304]{2,1,0:T(8,128)(2,1)} %all-gather.2.cloned.1.call-done) | copy-start | bytes 28311556
  129.0 250.6 %all-reduce.6.cloned.1.call-start = ((), (), s32[]{:S(2)}) async-start(), calls=%async_computation.4 | async-start | bytes 10616832 | tf_op jit(solution)/shard_map/psum | solution.py:42
  248.0 9.0 %slice-start = ((s8[9437184]{0:T(1024)(128)(4,1)}), s8[4194304]{0:T(1024)(128)(4,1)S(1)}, s32[]{:S(2)}) async-start(s8[9437184]{0:T(1024)(128)(4,1)} %bitcast.21), calls=%async_computation.5 | async-start | bytes 8388608
  249.6 7.4 %copy-start.2 = (bf16[1024,576]{0,1:T(8,128)(2,1)}, bf16[1024,576]{0,1:T(8,128)(2,1)S(1)}, u32[]{:S(2)}) copy-start(bf16[1024,576]{0,1:T(8,128)(2,1)S(1)} %fusion.8) | copy-start | bytes 3538948
  249.6 7.4 %slice-start.1 = ((s8[9437184]{0:T(1024)(128)(4,1)}), s8[4194304]{0:T(1024)(128)(4,1)S(1)}, s32[]{:S(2)}) async-start(s8[9437184]{0:T(1024)(128)(4,1)} %bitcast.21), calls=%async_computation.6 | async-start | bytes 8388608
  249.6 7.4 %slice-start.2 = ((s8[9437184]{0:T(1024)(128)(4,1)}), s8[1048576]{0:T(1024)(128)(4,1)S(1)}, s32[]{:S(2)}) async-start(s8[9437184]{0:T(1024)(128)(4,1)} %bitcast.21), calls=%async_computation.7 | async-start | bytes 2097152
  261.3 180.8 %reduce-scatter.2.cloned.1.call-start = ((), (), s32[]{:S(2)}) async-start(), calls=%async_computation.3 | async-start | bytes 5308416 | tf_op jit(solution)/shard_map/reduce_scatter | solution.py:27
  442.1 3.6 copy-start.1
Sparse Core Ops, SparseCore 0:
  10.4 107.7 all-gather.1
  129.1 116.6 all-reduce.3
  261.4 118.1 all-reduce.5
  382.8 59.2 reduce-scatter.1
where the time goes:
time: 454 us
  waiting for transfers between devices  399 us (88%)
  matrix products  27.9 us (6%)
  between operations  13.9 us (3%)
  other arithmetic  7.89 us (2%)
  local copies, waits for them, and re-layouts  5.11 us (1%)
    psum x1, waiting for transfers between devices, shards(): lax.psum(partial_sums.astype(jnp.bfloat16), 'col').astype(jnp.float32)  117 us
    psum x1, waiting for transfers between devices, shards(): lax.psum(acc_in.astype(jnp.bfloat16), 'rep').astype(jnp.float32)  111 us
    all_gather x1, waiting for transfers between devices, shards(): gathered = lax.all_gather(stacked, 'blk', axis=1, tiled=True)  108 us
    reduce_scatter x1, waiting for transfers between devices, shards(): lax.psum_scatter(jnp.einsum('tf,df->td', grad_pre, w_in, preferred_elemen...  62.5 us
  transfers between devices with their start and end apart: 4, of which 4 were waited for; matrix products, arithmetic and copies ran while one was open for 2% of the time, Pallas kernels for 0%

commit v1 on v0

v1 whole, which is shorter than its diff:
```python
import functools
import math

import jax
import jax.numpy as jnp
from jax import lax
from jax.experimental import pallas as pl
from jax.experimental.pallas import tpu as pltpu
from jax.sharding import PartitionSpec as P

MESH = pl.DeviceIdType.MESH
F32, BF16 = jnp.float32, jnp.bfloat16
NB, NC = 8, 8
TD, HALF, SUB, RC = 128, 64, 32, 16
DL, FL = 2304, 576
DH = DL // 2
YJ = 3
CO, RI = DH // YJ, DH // YJ
HO, HI = FL // 2, RI // 2
GELU_C = math.sqrt(2.0 / math.pi)
GELU_A = 0.044715
Y_LEAD = 3


def dot_nn(a, b):
    return jnp.dot(a, b, preferred_element_type=F32)


def dot_nt(a, b):
    return lax.dot_general(a, b, (((1,), (1,)), ((), ())), preferred_element_type=F32)


def gelu(v):
    return 0.5 * v * (1.0 + jnp.tanh(GELU_C * (v + GELU_A * (v * v * v))))


def gelu_grad(v):
    th = jnp.tanh(GELU_C * (v + GELU_A * (v * v * v)))
    slope = GELU_C * (1.0 + (3.0 * GELU_A) * (v * v))
    return 0.5 * (1.0 + th) + 0.5 * v * (1.0 - th * th) * slope


def kernel(
    scale,
    tokens,
    grad_out,
    w_in,
    w_out,
    gt_out,
    gi_out,
    go_out,
    xs,
    wi,
    wo,
    tok_t,
    hid_t,
    act,
    part,
    share,
    pre,
    zst,
    zrb,
    gst,
    ss_o,
    sr_o,
    own_o,
    ys_o,
    yr_o,
    fin_o,
    ss_i,
    sr_i,
    own_i,
    ys_i,
    yr_i,
    fin_i,
    load_sem,
    zsend,
    zrecv,
    rs_send,
    rs_recv,
    ag_send,
    ag_recv,
    qsend,
    qrecv,
    ysem,
    out_sem,
    gt_sem,
):
    b, c, r = lax.axis_index("blk"), lax.axis_index("col"), lax.axis_index("rep")
    yh, core = r // 2, r % 2
    up, down = lax.rem(b + 1, NB), lax.rem(b + NB - 1, NB)
    ring = ((up, c, r), (down, c, r))
    sibling = (b, c, yh * 2 + (1 - core))
    partner = (b, c, (1 - yh) * 2 + core)

    def col_partner(k):
        return lax.rem(c + k, NC)

    loads = [
        pltpu.make_async_copy(tokens, xs.at[0, pl.ds(0, TD)], load_sem.at[0]),
        pltpu.make_async_copy(w_in, wi, load_sem.at[1]),
        pltpu.make_async_copy(grad_out, xs.at[1, pl.ds(0, TD)], load_sem.at[2]),
        pltpu.make_async_copy(w_out, wo, load_sem.at[3]),
    ]
    for copy in loads:
        copy.start()

    barrier = pltpu.get_barrier_semaphore()
    peers = list(ring) + [sibling, partner]
    peers += [(b, col_partner(k), r) for k in range(1, NC)]
    for peer in peers:
        pl.semaphore_signal(barrier, inc=1, device_id=peer, device_id_type=MESH)
    pl.semaphore_wait(barrier, len(peers))

    def hop(t, s, d, q):
        rows = d * HALF + q * SUB
        return pltpu.make_async_remote_copy(
            src_ref=xs.at[t, pl.ds(s * TD + rows, SUB)],
            dst_ref=xs.at[t, pl.ds((s + 1) * TD + rows, SUB)],
            send_sem=zsend.at[t, s, d, q],
            recv_sem=zrecv.at[t, s, d, q],
            device_id=ring[d],
            device_id_type=MESH,
        )

    def pass_on(t, s):
        for q in range(2):
            for d in range(2):
                hop(t, s - 1, d, q).wait_recv()

                @pl.when(s < NB - 1)
                def _():
                    hop(t, s, d, q).start()

    def rs_copy(t, s, k):
        p = col_partner(k)
        return pltpu.make_async_remote_copy(
            src_ref=part.at[t, s, pl.ds(p * RC, RC)],
            dst_ref=share.at[t, s, k - 1],
            send_sem=rs_send.at[t, s],
            recv_sem=rs_recv.at[t, s],
            device_id=(b, p, r),
            device_id_type=MESH,
        )

    def ag_copy(t, s, k):
        rows = pl.ds(s * TD + c * RC, RC)
        return pltpu.make_async_remote_copy(
            src_ref=act.at[t, rows],
            dst_ref=act.at[t, rows],
            send_sem=ag_send.at[t, s],
            recv_sem=ag_recv.at[t, s],
            device_id=(b, col_partner(k), r),
            device_id_type=MESH,
        )

    def wait_bytes(sem, ref):
        pltpu.make_async_copy(ref, ref, sem).wait()

    def multiply(t, s):
        x = xs[t, pl.ds(s * TD, TD)]
        p = dot_nn(x, wi[...]) if t == 0 else dot_nt(x, wo[...])
        part[t, s] = p.astype(BF16)
        for k in range(1, NC):
            rs_copy(t, s, k).start()

    def reduce(t, s):
        wait_bytes(rs_recv.at[t, s], share.at[t, s])
        total = part[t, s, pl.ds(c * RC, RC)].astype(F32)
        for k in range(NC - 1):
            total += share[t, s, k].astype(F32)
        if t == 0:
            pre[s] = total
            value = gelu(total)
        else:
            value = total * gelu_grad(pre[s])
        act[t, pl.ds(s * TD + c * RC, RC)] = value.astype(BF16)
        for k in range(1, NC):
            ag_copy(t, s, k).start()

    def arrived(t, s):
        wait_bytes(ag_recv.at[t, s], act.at[t, pl.ds(s * TD, (NC - 1) * RC)])
        if t == 0:
            cols = pl.ds(pl.multiple_of(s * TD, TD), TD)
            hid_t[:, cols] = act[t, pl.ds(s * TD, TD)].T

    def transpose_tokens(s):
        cols = pl.ds(pl.multiple_of(s * TD, TD), TD)
        tok_t[:, cols] = xs[0, pl.ds(s * TD, TD)].T

    loads[0].wait()
    for q in range(2):
        for d in range(2):
            hop(0, 0, d, q).start()
        if q == 0:
            for d in range(2):
                hop(0, 0, d, q).wait_send()
    loads[1].wait()
    loads[2].wait()

    def tokens_step(s, carry):
        @pl.when(s > 0)
        def _():
            pass_on(0, s)

        @pl.when(s == NB - 2)
        def _():
            for q in range(2):
                for d in range(2):
                    hop(1, 0, d, q).start()

        multiply(0, s)

        @pl.when(s > 0)
        def _():
            reduce(0, s - 1)

        @pl.when(s > 1)
        def _():
            arrived(0, s - 2)

        transpose_tokens(s)
        return carry

    lax.fori_loop(0, NB, tokens_step, 0)
    loads[3].wait()

    def grads_step(s, carry):
        @pl.when(s > 0)
        def _():
            pass_on(1, s)

        multiply(1, s)

        @pl.when(s == 0)
        def _():
            reduce(0, NB - 1)
            arrived(0, NB - 2)

        @pl.when(s == 1)
        def _():
            arrived(0, NB - 1)

        @pl.when(s > 0)
        def _():
            reduce(1, s - 1)

        @pl.when(s > 1)
        def _():
            arrived(1, s - 2)

        return carry

    lax.fori_loop(0, NB, grads_step, 0)

    kinds = (
        (ss_o, sr_o, own_o, ys_o, yr_o, fin_o, HO),
        (ss_i, sr_i, own_i, ys_i, yr_i, fin_i, HI),
    )

    def remote(src, dst, sems, device):
        return pltpu.make_async_remote_copy(
            src_ref=src,
            dst_ref=dst,
            send_sem=sems.at[0],
            recv_sem=sems.at[1],
            device_id=device,
            device_id_type=MESH,
        )

    def core_copy(n, j):
        return remote(kinds[n][0].at[j], kinds[n][1].at[j], ysem.at[n, j, 0], sibling)

    def y_copy(n, j):
        return remote(kinds[n][3].at[j], kinds[n][4].at[j], ysem.at[n, j, 1], partner)

    def fin_copy(n, j, which):
        fin, h = kinds[n][5], kinds[n][6]
        half = (1 - yh) if which == 2 else yh
        ref = fin.at[core, j, pl.ds(half * h, h)]
        return remote(ref, ref, ysem.at[n, j, 2 + which], partner if which == 0 else sibling)

    def block(n, j, k):
        if n == 0:
            cols = pl.ds(pl.multiple_of(k * DH + j * CO, 128), CO)
            return dot_nn(hid_t[...], xs[1, :, cols]) * scale
        return dot_nn(tok_t[pl.ds(k * DH + j * RI, RI)], act[1]) * scale

    def y_start(n, j):
        ss, _, own = kinds[n][:3]
        ss[j] = block(n, j, 1 - core).astype(BF16)
        core_copy(n, j).start()
        own[j] = block(n, j, core)

    def y_middle(n, j):
        _, sr, own, ys, _, _, h = kinds[n]
        core_copy(n, j).wait_recv()
        theirs, mine = pl.ds((1 - yh) * h, h), pl.ds(yh * h, h)
        ys[j] = (own[j, theirs] + sr[j, theirs].astype(F32)).astype(BF16)
        y_copy(n, j).start()
        own[j, mine] = own[j, mine] + sr[j, mine].astype(F32)

    def y_final(n, j):
        _, _, own, _, yr, fin, h = kinds[n]
        y_copy(n, j).wait_recv()
        mine = pl.ds(yh * h, h)
        fin[core, j, mine] = (own[j, mine] + yr[j].astype(F32)).astype(BF16)
        fin_copy(n, j, 0).start()
        fin_copy(n, j, 1).start()

    def out_copy(n, j, k):
        if n == 0:
            cols = pl.ds(pl.multiple_of(k * DH + j * CO, 128), CO)
            return pltpu.make_async_copy(fin_o.at[k, j], go_out.at[:, cols], out_sem.at[n, j, k])
        return pltpu.make_async_copy(fin_i.at[k, j], gi_out.at[pl.ds(k * DH + j * RI, RI)], out_sem.at[n, j, k])

    def y_forward(n, j):
        fin_copy(n, j, 0).wait_recv()
        fin_copy(n, j, 2).start()
        out_copy(n, j, core).start()

    def y_end(n, j):
        fin_copy(n, j, 1).wait_recv()
        fin_copy(n, j, 2).wait_recv()
        out_copy(n, j, 1 - core).start()

    def at_tile(step, j):
        for n in range(2):

            @pl.when((j >= n * YJ) & (j < (n + 1) * YJ))
            def _():
                step(n, j - n * YJ)

    def z_copy(k, h, d):
        rows = pl.ds(d * HALF, HALF)
        return pltpu.make_async_remote_copy(
            src_ref=zst.at[k, h, rows],
            dst_ref=zrb.at[k, h, rows],
            send_sem=qsend.at[k, h, d],
            recv_sem=qrecv.at[k, h, d],
            device_id=ring[1 - d],
            device_id_type=MESH,
        )

    def gt_copy(h):
        return pltpu.make_async_copy(gst.at[h], gt_out.at[:, pl.ds(h * DH, DH)], gt_sem.at[h])

    def z_slot(i):
        k, h = i // 2, i % 2
        s = NB - 1 - k
        value = dot_nt(act[1, pl.ds(s * TD, TD)], wi[pl.ds(h * DH, DH)])

        @pl.when(k == 0)
        def _():
            zst[k, h] = value.astype(BF16)

        @pl.when((k > 0) & (k < NB - 1))
        def _():
            for d in range(2):
                z_copy(k - 1, h, d).wait_recv()
            zst[k, h] = (value + zrb[k - 1, h].astype(F32)).astype(BF16)

        @pl.when(k < NB - 1)
        def _():
            for d in range(2):
                z_copy(k, h, d).start()

        @pl.when(k == NB - 1)
        def _():
            for d in range(2):
                z_copy(k - 1, h, d).wait_recv()
            gst[h] = (value + zrb[k - 1, h].astype(F32)).astype(BF16)

    def slot(g, carry):
        @pl.when(g == 1)
        def _():
            reduce(1, NB - 1)

        @pl.when(g == 2)
        def _():
            arrived(1, NB - 2)
            arrived(1, NB - 1)

        i = g - Y_LEAD

        @pl.when((i >= 0) & (i < 2 * NB))
        def _():
            z_slot(i)

        j = g // 3

        @pl.when(g % 3 == 0)
        def _():
            at_tile(y_start, j)

        @pl.when(g % 3 == 1)
        def _():
            at_tile(y_middle, j)

        @pl.when(g % 3 == 2)
        def _():
            at_tile(y_final, j - 1)
            at_tile(y_forward, j - 2)
            at_tile(y_end, j - 3)

        return carry

    lax.fori_loop(0, 3 * (2 * YJ + 3), slot, 0)
    for h in range(2):
        gt_copy(h).start()

    for h in range(2):
        gt_copy(h).wait()

    def drain_tiles(j, carry):
        for n in range(2):
            core_copy(n, j).wait_send()
            y_copy(n, j).wait_send()
            for which in range(3):
                fin_copy(n, j, which).wait_send()
            for k in range(2):
                out_copy(n, j, k).wait()
        return carry

    lax.fori_loop(0, YJ, drain_tiles, 0)

    def drain_hops(s, carry):
        for d in range(2):
            for q in range(2):
                for t in range(2):
                    if t == 0 and q == 0:

                        @pl.when(s > 0)
                        def _():
                            hop(t, s, d, q).wait_send()
                    else:
                        hop(t, s, d, q).wait_send()
                z_copy(s, q, d).wait_send()
        return carry

    lax.fori_loop(0, NB - 1, drain_hops, 0)

    def drain_sums(s, carry):
        for t in range(2):
            wait_bytes(rs_send.at[t, s], share.at[t, s])
            wait_bytes(ag_send.at[t, s], share.at[t, s])
        return carry

    lax.fori_loop(0, NB, drain_sums, 0)


def shards(tokens, grad_out, w_in, w_out):
    total_tokens = tokens.shape[0] * lax.axis_size("blk") * lax.axis_size("rep")
    scale = 1.0 / math.sqrt(total_tokens)
    any_space = pl.BlockSpec(memory_space=pl.ANY)
    dma = pltpu.SemaphoreType.DMA
    rows = NB * TD
    flops = 10 * rows * DL * FL
    return pl.pallas_call(
        functools.partial(kernel, scale),
        out_shape=(
            jax.ShapeDtypeStruct((TD, DL), BF16),
            jax.ShapeDtypeStruct((DL, FL), BF16),
            jax.ShapeDtypeStruct((FL, DL), BF16),
        ),
        in_specs=[any_space] * 4,
        out_specs=(any_space,) * 3,
        scratch_shapes=[
            pltpu.VMEM((2, rows, DL), BF16),
            pltpu.VMEM((DL, FL), BF16),
            pltpu.VMEM((FL, DL), BF16),
            pltpu.VMEM((DL, rows), BF16),
            pltpu.VMEM((FL, rows), BF16),
            pltpu.VMEM((2, rows, FL), BF16),
            pltpu.VMEM((2, NB, TD, FL), BF16),
            pltpu.VMEM((2, NB, NC - 1, RC, FL), BF16),
            pltpu.VMEM((NB, RC, FL), F32),
            pltpu.VMEM((NB - 1, 2, TD, DH), BF16),
            pltpu.VMEM((NB - 1, 2, TD, DH), BF16),
            pltpu.VMEM((2, TD, DH), BF16),
            pltpu.VMEM((YJ, FL, CO), BF16),
            pltpu.VMEM((YJ, FL, CO), BF16),
            pltpu.VMEM((YJ, FL, CO), F32),
            pltpu.VMEM((YJ, HO, CO), BF16),
            pltpu.VMEM((YJ, HO, CO), BF16),
            pltpu.VMEM((2, YJ, FL, CO), BF16),
            pltpu.VMEM((YJ, RI, FL), BF16),
            pltpu.VMEM((YJ, RI, FL), BF16),
            pltpu.VMEM((YJ, RI, FL), F32),
            pltpu.VMEM((YJ, HI, FL), BF16),
            pltpu.VMEM((YJ, HI, FL), BF16),
            pltpu.VMEM((2, YJ, RI, FL), BF16),
            dma((4,)),
            dma((2, NB - 1, 2, 2)),
            dma((2, NB - 1, 2, 2)),
            dma((2, NB)),
            dma((2, NB)),
            dma((2, NB)),
            dma((2, NB)),
            dma((NB - 1, 2, 2)),
            dma((NB - 1, 2, 2)),
            dma((2, YJ, 5, 2)),
            dma((2, YJ, 2)),
            dma((2,)),
        ],
        compiler_params=pltpu.CompilerParams(
            collective_id=0, has_side_effects=True, vmem_limit_bytes=62 * 2**20
        ),
        cost_estimate=pl.CostEstimate(
            flops=flops, bytes_accessed=16 * 2**20, transcendentals=4 * rows * FL // NC
        ),
    )(tokens, grad_out, w_in, w_out)


def solution(mesh):
    placed = (P(("blk", "rep"), "col"), P(("blk", "rep"), "col"), P("col", "blk"), P("blk", "col"))
    return jax.shard_map(
        shards,
        mesh=mesh,
        in_specs=placed,
        out_specs=(P(("blk", "rep"), "col"), P("col", "blk"), P("blk", "col")),
        check_vma=False,
    )
```

time: 454 us -> 192 us (0.42)
  waiting for transfers between devices: 399 us -> 0 us
  Pallas kernels: 0 us -> 179 us
  matrix products: 27.9 us -> 0 us
  between operations: 13.9 us -> 0.66 us
  other arithmetic: 7.89 us -> 0 us
  local copies, waits for them, and re-layouts: 5.11 us -> 11.5 us
    psum x2 -> x0, waiting for transfers between devices: 228 us -> none  [the longest x1 117 us: shards(): lax.psum(partial_sums.astype(jnp.bfloat16), 'col').astype(jnp.float32)]
    pallas_call x0 -> x1, Pallas kernels: none -> 179 us  [shards(): pl.pallas_call(functools.partial(kernel, scale), out_shape=(jax.ShapeDtyp...]
    all_gather x1 -> x0, waiting for transfers between devices: 108 us -> none  [shards(): gathered = lax.all_gather(stacked, 'blk', axis=1, tiled=True)]
    reduce_scatter x1 -> x0, waiting for transfers between devices: 62.5 us -> none  [shards(): lax.psum_scatter(jnp.einsum('tf,df->td', grad_pre, w_in, preferred_elemen...]
    dot_general x5 -> x0, matrix products: 27.9 us -> none  [the longest x1 7.36 us: shards(): jnp.einsum('tf,td->fd', hidden, gathered[1], preferred_element_type=jnp.f...]
    pallas_call x0 -> x1, local copies, waits for them, and re-layouts: none -> 4.64 us  [shards(): pl.pallas_call(functools.partial(kernel, scale), out_shape=(jax.ShapeDtyp...]
  transfers between devices with their start and end apart: 4 -> 0, of which waited for: 4 -> 0; matrix products, arithmetic and copies ran while one was open for 2% -> 0% of each run, Pallas kernels for 0% -> 0%
where the time goes in v1:
time: 192 us
  Pallas kernels  179 us (93%)
  local copies, waits for them, and re-layouts  11.5 us (6%)
    pallas_call x1, Pallas kernels, shards(): pl.pallas_call(functools.partial(kernel, scale), out_shape=(jax.ShapeDtyp...  179 us
    unnamed x7, local copies, waits for them, and re-layouts  6.83 us
    pallas_call x1, local copies, waits for them, and re-layouts, shards(): pl.pallas_call(functools.partial(kernel, scale), out_shape=(jax.ShapeDtyp...  4.64 us

profile of v1, /device:TPU:1, one launch (start us, length us, event | category | flops | bytes accessed | tf_op | source)
XLA Modules:
  0.0 191.5 jit_solution(4508279151012215019)
XLA Ops:
  0.6 4.5 %copy.7.w_in = bf16[2304,576]{1,0:T(8,128)(2,1)} copy(bf16[2304,576]{0,1:T(8,128)(2,1)} %param.6) | data formatting | bytes 5308416 | tf_op args[2]
  5.1 179.4 %shard_map.67 = (bf16[128,2304]{1,0:T(8,128)(2,1)}, bf16[2304,576]{1,0:T(8,128)(2,1)}, bf16[576,2304]{1,0:T(8,128)(2,1)}) custom-call(bf16[128,2304]{1,0:T(8,128)(2,1)} %tokens.1, bf16[128,2304]{1,0:T(8,128)(2,1)} %grad_out.1, bf16[2304,576]{1,0:T(8,128)(2,1)} %copy.7.w_in, bf16[576,2304]{1,0:T(8,128)(2,1)} %w_out.1), custom_call_target="tpu_custom_call" | custom-call | flops 13589544960 | bytes 16777216 | tf_op jit(solution)/shard_map/pallas_call | solution.py:459
  184.5 0.0 copy-start.1
  184.6 0.0 copy-start
  184.6 4.6 %copy.8 = bf16[2304,576]{0,1:T(8,128)(2,1)} copy(bf16[2304,576]{1,0:T(8,128)(2,1)} %get-tuple-element.4) | data formatting | bytes 5308416 | tf_op jit(solution)/shard_map/pallas_call | solution.py:459
  189.2 0.0 copy-done.1
  189.2 0.8 copy.11
  190.0 0.0 copy-done
  190.0 1.5 copy.12
Async XLA Ops:
  184.5 4.7 %copy-start.1 = (bf16[128,2304]{1,0:T(8,128)(2,1)S(1)}, bf16[128,2304]{1,0:T(8,128)(2,1)}, u32[]{:S(2)}) copy-start(bf16[128,2304]{1,0:T(8,128)(2,1)} %get-tuple-element.9) | copy-start | bytes 1769476
  184.6 5.5 %copy-start = (bf16[576,2304]{1,0:T(8,128)(2,1)S(1)}, bf16[576,2304]{1,0:T(8,128)(2,1)}, u32[]{:S(2)}) copy-start(bf16[576,2304]{1,0:T(8,128)(2,1)} %get-tuple-element.11) | copy-start | bytes 7962628

commit v2 on v1

--- a/solution.py
+++ b/solution.py
@@ -15,8 +15,7 @@
 DL, FL = 2304, 576
 DH = DL // 2
 YJ = 3
-CO, RI = DH // YJ, DH // YJ
-HO, HI = FL // 2, RI // 2
+TC = DH // YJ
 GELU_C = math.sqrt(2.0 / math.pi)
 GELU_A = 0.044715
 Y_LEAD = 3
@@ -44,35 +43,25 @@
     scale,
     tokens,
     grad_out,
-    w_in,
+    w_in_t,
     w_out,
     gt_out,
     gi_out,
     go_out,
     xs,
-    wi,
-    wo,
-    tok_t,
-    hid_t,
+    w,
+    act_t,
     act,
     part,
     share,
     pre,
     zst,
     zrb,
-    gst,
-    ss_o,
-    sr_o,
-    own_o,
-    ys_o,
-    yr_o,
-    fin_o,
-    ss_i,
-    sr_i,
-    own_i,
-    ys_i,
-    yr_i,
-    fin_i,
+    ss,
+    sr,
+    own,
+    ys,
+    yr,
     load_sem,
     zsend,
     zrecv,
@@ -83,8 +72,6 @@
     qsend,
     qrecv,
     ysem,
-    out_sem,
-    gt_sem,
 ):
     b, c, r = lax.axis_index("blk"), lax.axis_index("col"), lax.axis_index("rep")
     yh, core = r // 2, r % 2
@@ -98,9 +85,9 @@
 
     loads = [
         pltpu.make_async_copy(tokens, xs.at[0, pl.ds(0, TD)], load_sem.at[0]),
-        pltpu.make_async_copy(w_in, wi, load_sem.at[1]),
+        pltpu.make_async_copy(w_in_t, w.at[0], load_sem.at[1]),
         pltpu.make_async_copy(grad_out, xs.at[1, pl.ds(0, TD)], load_sem.at[2]),
-        pltpu.make_async_copy(w_out, wo, load_sem.at[3]),
+        pltpu.make_async_copy(w_out, w.at[1], load_sem.at[3]),
     ]
     for copy in loads:
         copy.start()
@@ -159,8 +146,7 @@
 
     def multiply(t, s):
         x = xs[t, pl.ds(s * TD, TD)]
-        p = dot_nn(x, wi[...]) if t == 0 else dot_nt(x, wo[...])
-        part[t, s] = p.astype(BF16)
+        part[t, s] = dot_nt(x, w[t]).astype(BF16)
         for k in range(1, NC):
             rs_copy(t, s, k).start()
 
@@ -180,13 +166,8 @@
 
     def arrived(t, s):
         wait_bytes(ag_recv.at[t, s], act.at[t, pl.ds(s * TD, (NC - 1) * RC)])
-        if t == 0:
-            cols = pl.ds(pl.multiple_of(s * TD, TD), TD)
-            hid_t[:, cols] = act[t, pl.ds(s * TD, TD)].T
-
-    def transpose_tokens(s):
         cols = pl.ds(pl.multiple_of(s * TD, TD), TD)
-        tok_t[:, cols] = xs[0, pl.ds(s * TD, TD)].T
+        act_t[t, :, cols] = act[t, pl.ds(s * TD, TD)].T
 
     loads[0].wait()
     for q in range(2):
@@ -219,7 +200,6 @@
         def _():
             arrived(0, s - 2)
 
-        transpose_tokens(s)
         return carry
 
     lax.fori_loop(0, NB, tokens_step, 0)
@@ -252,11 +232,6 @@
         return carry
 
     lax.fori_loop(0, NB, grads_step, 0)
-
-    kinds = (
-        (ss_o, sr_o, own_o, ys_o, yr_o, fin_o, HO),
-        (ss_i, sr_i, own_i, ys_i, yr_i, fin_i, HI),
-    )
 
     def remote(src, dst, sems, device):
         return pltpu.make_async_remote_copy(
@@ -268,61 +243,42 @@
             device_id_type=MESH,
         )
 
+    fin = (go_out, gi_out)
+
     def core_copy(n, j):
-        return remote(kinds[n][0].at[j], kinds[n][1].at[j], ysem.at[n, j, 0], sibling)
+        return remote(ss.at[n, j], sr.at[n, j], ysem.at[n, j, 0], sibling)
 
     def y_copy(n, j):
-        return remote(kinds[n][3].at[j], kinds[n][4].at[j], ysem.at[n, j, 1], partner)
-
-    def fin_copy(n, j, which):
-        fin, h = kinds[n][5], kinds[n][6]
-        half = (1 - yh) if which == 2 else yh
-        ref = fin.at[core, j, pl.ds(half * h, h)]
-        return remote(ref, ref, ysem.at[n, j, 2 + which], partner if which == 0 else sibling)
+        return remote(ys.at[n, j], yr.at[n, j], ysem.at[n, j, 1], partner)
+
+    def tile_cols(j, k):
+        return pl.ds(pl.multiple_of(k * DH + j * TC, 128), TC)
+
+    def fin_copy(n, j):
+        ref = fin[n].at[:, tile_cols(j, core)]
+        return remote(ref, ref, ysem.at[n, j, 2], sibling)
 
     def block(n, j, k):
-        if n == 0:
-            cols = pl.ds(pl.multiple_of(k * DH + j * CO, 128), CO)
-            return dot_nn(hid_t[...], xs[1, :, cols]) * scale
-        return dot_nn(tok_t[pl.ds(k * DH + j * RI, RI)], act[1]) * scale
+        return dot_nn(act_t[n], xs[1 - n, :, tile_cols(j, k)]) * scale
 
     def y_start(n, j):
-        ss, _, own = kinds[n][:3]
-        ss[j] = block(n, j, 1 - core).astype(BF16)
+        ss[n, j] = block(n, j, 1 - core).astype(BF16)
         core_copy(n, j).start()
-        own[j] = block(n, j, core)
+        own[n, j] = block(n, j, core)
 
     def y_middle(n, j):
-        _, sr, own, ys, _, _, h = kinds[n]
         core_copy(n, j).wait_recv()
-        theirs, mine = pl.ds((1 - yh) * h, h), pl.ds(yh * h, h)
-        ys[j] = (own[j, theirs] + sr[j, theirs].astype(F32)).astype(BF16)
+        ys[n, j] = (own[n, j] + sr[n, j].astype(F32)).astype(BF16)
         y_copy(n, j).start()
-        own[j, mine] = own[j, mine] + sr[j, mine].astype(F32)
 
     def y_final(n, j):
-        _, _, own, _, yr, fin, h = kinds[n]
         y_copy(n, j).wait_recv()
-        mine = pl.ds(yh * h, h)
-        fin[core, j, mine] = (own[j, mine] + yr[j].astype(F32)).astype(BF16)
-        fin_copy(n, j, 0).start()
-        fin_copy(n, j, 1).start()
-
-    def out_copy(n, j, k):
-        if n == 0:
-            cols = pl.ds(pl.multiple_of(k * DH + j * CO, 128), CO)
-            return pltpu.make_async_copy(fin_o.at[k, j], go_out.at[:, cols], out_sem.at[n, j, k])
-        return pltpu.make_async_copy(fin_i.at[k, j], gi_out.at[pl.ds(k * DH + j * RI, RI)], out_sem.at[n, j, k])
-
-    def y_forward(n, j):
-        fin_copy(n, j, 0).wait_recv()
-        fin_copy(n, j, 2).start()
-        out_copy(n, j, core).start()
+        value = (ys[n, j].astype(F32) + yr[n, j].astype(F32)).astype(BF16)
+        fin[n][:, tile_cols(j, core)] = value
+        fin_copy(n, j).start()
 
     def y_end(n, j):
-        fin_copy(n, j, 1).wait_recv()
-        fin_copy(n, j, 2).wait_recv()
-        out_copy(n, j, 1 - core).start()
+        fin_copy(n, j).wait_recv()
 
     def at_tile(step, j):
         for n in range(2):
@@ -342,13 +298,10 @@
             device_id_type=MESH,
         )
 
-    def gt_copy(h):
-        return pltpu.make_async_copy(gst.at[h], gt_out.at[:, pl.ds(h * DH, DH)], gt_sem.at[h])
-
     def z_slot(i):
         k, h = i // 2, i % 2
         s = NB - 1 - k
-        value = dot_nt(act[1, pl.ds(s * TD, TD)], wi[pl.ds(h * DH, DH)])
+        value = dot_nn(act[1, pl.ds(s * TD, TD)], w[0, :, pl.ds(pl.multiple_of(h * DH, 128), DH)])
 
         @pl.when(k == 0)
         def _():
@@ -369,7 +322,7 @@
         def _():
             for d in range(2):
                 z_copy(k - 1, h, d).wait_recv()
-            gst[h] = (value + zrb[k - 1, h].astype(F32)).astype(BF16)
+            gt_out[:, pl.ds(pl.multiple_of(h * DH, 128), DH)] = (value + zrb[k - 1, h].astype(F32)).astype(BF16)
 
     def slot(g, carry):
         @pl.when(g == 1)
@@ -400,26 +353,18 @@
         @pl.when(g % 3 == 2)
         def _():
             at_tile(y_final, j - 1)
-            at_tile(y_forward, j - 2)
-            at_tile(y_end, j - 3)
-
-        return carry
-
-    lax.fori_loop(0, 3 * (2 * YJ + 3), slot, 0)
-    for h in range(2):
-        gt_copy(h).start()
-
-    for h in range(2):
-        gt_copy(h).wait()
+            at_tile(y_end, j - 2)
+
+        return carry
+
+    lax.fori_loop(0, 3 * (2 * YJ + 2), slot, 0)
+
 
     def drain_tiles(j, carry):
         for n in range(2):
             core_copy(n, j).wait_send()
             y_copy(n, j).wait_send()
-            for which in range(3):
-                fin_copy(n, j, which).wait_send()
-            for k in range(2):
-                out_copy(n, j, k).wait()
+            fin_copy(n, j).wait_send()
         return carry
 
     lax.fori_loop(0, YJ, drain_tiles, 0)
@@ -456,40 +401,30 @@
     dma = pltpu.SemaphoreType.DMA
     rows = NB * TD
     flops = 10 * rows * DL * FL
-    return pl.pallas_call(
+    grad_tokens, grad_in_t, grad_outw = pl.pallas_call(
         functools.partial(kernel, scale),
         out_shape=(
-            jax.ShapeDtypeStruct((TD, DL), BF16),
-            jax.ShapeDtypeStruct((DL, FL), BF16),
-            jax.ShapeDtypeStruct((FL, DL), BF16),
+            pltpu.VMEM((TD, DL), BF16),
+            pltpu.VMEM((FL, DL), BF16),
+            pltpu.VMEM((FL, DL), BF16),
         ),
         in_specs=[any_space] * 4,
-        out_specs=(any_space,) * 3,
+        out_specs=(pl.BlockSpec(memory_space=pltpu.VMEM),) * 3,
         scratch_shapes=[
             pltpu.VMEM((2, rows, DL), BF16),
-            pltpu.VMEM((DL, FL), BF16),
-            pltpu.VMEM((FL, DL), BF16),
-            pltpu.VMEM((DL, rows), BF16),
-            pltpu.VMEM((FL, rows), BF16),
+            pltpu.VMEM((2, FL, DL), BF16),
+            pltpu.VMEM((2, FL, rows), BF16),
             pltpu.VMEM((2, rows, FL), BF16),
             pltpu.VMEM((2, NB, TD, FL), BF16),
             pltpu.VMEM((2, NB, NC - 1, RC, FL), BF16),
             pltpu.VMEM((NB, RC, FL), F32),
             pltpu.VMEM((NB - 1, 2, TD, DH), BF16),
             pltpu.VMEM((NB - 1, 2, TD, DH), BF16),
-            pltpu.VMEM((2, TD, DH), BF16),
-            pltpu.VMEM((YJ, FL, CO), BF16),
-            pltpu.VMEM((YJ, FL, CO), BF16),
-            pltpu.VMEM((YJ, FL, CO), F32),
-            pltpu.VMEM((YJ, HO, CO), BF16),
-            pltpu.VMEM((YJ, HO, CO), BF16),
-            pltpu.VMEM((2, YJ, FL, CO), BF16),
-            pltpu.VMEM((YJ, RI, FL), BF16),
-            pltpu.VMEM((YJ, RI, FL), BF16),
-            pltpu.VMEM((YJ, RI, FL), F32),
-            pltpu.VMEM((YJ, HI, FL), BF16),
-            pltpu.VMEM((YJ, HI, FL), BF16),
-            pltpu.VMEM((2, YJ, RI, FL), BF16),
+            pltpu.VMEM((2, YJ, FL, TC), BF16),
+            pltpu.VMEM((2, YJ, FL, TC), BF16),
+            pltpu.VMEM((2, YJ, FL, TC), F32),
+            pltpu.VMEM((2, YJ, FL, TC), BF16),
+            pltpu.VMEM((2, YJ, FL, TC), BF16),
             dma((4,)),
             dma((2, NB - 1, 2, 2)),
             dma((2, NB - 1, 2, 2)),
@@ -499,17 +434,16 @@
             dma((2, NB)),
             dma((NB - 1, 2, 2)),
             dma((NB - 1, 2, 2)),
-            dma((2, YJ, 5, 2)),
-            dma((2, YJ, 2)),
-            dma((2,)),
+            dma((2, YJ, 3, 2)),
         ],
         compiler_params=pltpu.CompilerParams(
-            collective_id=0, has_side_effects=True, vmem_limit_bytes=62 * 2**20
+            collective_id=0, has_side_effects=True, vmem_limit_bytes=56 * 2**20
         ),
         cost_estimate=pl.CostEstimate(
             flops=flops, bytes_accessed=16 * 2**20, transcendentals=4 * rows * FL // NC
         ),
-    )(tokens, grad_out, w_in, w_out)
+    )(tokens, grad_out, w_in.T, w_out)
+    return grad_tokens, grad_in_t.T, grad_outw
 
 
 def solution(mesh):

time: 192 us -> 177 us (0.922)
  local copies, waits for them, and re-layouts: 11.5 us -> 3.82 us
  Pallas kernels: 179 us -> 172 us
    pallas_call x1, Pallas kernels: 179 us -> 172 us  [shards(): pl.pallas_call(functools.partial(kernel, scale), out_shape=(pltpu.VMEM((T...]
    pallas_call x1 -> x0, local copies, waits for them, and re-layouts: 4.64 us -> none  [shards(): pl.pallas_call(functools.partial(kernel, scale), out_shape=(jax.ShapeDtyp...]
    unnamed x7 -> x3, local copies, waits for them, and re-layouts: 6.83 us -> 3.82 us
where the time goes in v2:
time: 177 us
  Pallas kernels  172 us (97%)
  local copies, waits for them, and re-layouts  3.82 us (2%)
    pallas_call x1, Pallas kernels, shards(): pl.pallas_call(functools.partial(kernel, scale), out_shape=(pltpu.VMEM((T...  172 us
    unnamed x3, local copies, waits for them, and re-layouts  3.82 us

profile of v2, /device:TPU:1, one launch (start us, length us, event | category | flops | bytes accessed | tf_op | source)
XLA Modules:
  0.0 176.7 jit_solution(3037851135445466217)
XLA Ops:
  0.6 172.3 %shard_map.67 = (bf16[128,2304]{1,0:T(8,128)(2,1)S(1)}, bf16[576,2304]{1,0:T(8,128)(2,1)S(1)}, bf16[576,2304]{1,0:T(8,128)(2,1)S(1)}) custom-call(bf16[128,2304]{1,0:T(8,128)(2,1)} %tokens.1, bf16[128,2304]{1,0:T(8,128)(2,1)} %grad_out.1, bf16[576,2304]{1,0:T(8,128)(2,1)} %bitcast.3, bf16[576,2304]{1,0:T(8,128)(2,1)} %w_out.1), custom_call_target="tpu_custom_call" | custom-call | flops 13589544960 | bytes 16777216 | tf_op jit(solution)/shard_map/pallas_call | solution.py:404
  172.9 0.8 copy.10
  173.7 1.5 copy.11
  175.2 1.5 copy.12

commit v3 on v2

--- a/solution.py
+++ b/solution.py
@@ -16,9 +16,19 @@
 DH = DL // 2
 YJ = 3
 TC = DH // YJ
+CW = 2 * TC
+PIECES = (
+    (0, pl.ds(0, SUB), pl.ds(0, DL)),
+    (0, pl.ds(SUB, SUB), pl.ds(0, DL)),
+    (1, pl.ds(0, SUB), pl.ds(0, DL)),
+    (1, pl.ds(SUB, SUB), pl.ds(0, DL)),
+)
+FIRST, SECOND = (0, 1), (2, 3)
 GELU_C = math.sqrt(2.0 / math.pi)
 GELU_A = 0.044715
-Y_LEAD = 3
+LAG_SUM, LAG_ACT = 2, 4
+LATE = 8
+Y_LEAD = 2
 
 
 def dot_nn(a, b):
@@ -99,25 +109,26 @@
         pl.semaphore_signal(barrier, inc=1, device_id=peer, device_id_type=MESH)
     pl.semaphore_wait(barrier, len(peers))
 
-    def hop(t, s, d, q):
-        rows = d * HALF + q * SUB
+    def hop(q, s, d):
+        t, rows, cols = PIECES[q]
+        start = d * HALF + rows.start
         return pltpu.make_async_remote_copy(
-            src_ref=xs.at[t, pl.ds(s * TD + rows, SUB)],
-            dst_ref=xs.at[t, pl.ds((s + 1) * TD + rows, SUB)],
-            send_sem=zsend.at[t, s, d, q],
-            recv_sem=zrecv.at[t, s, d, q],
+            src_ref=xs.at[t, pl.ds(s * TD + start, rows.size), cols],
+            dst_ref=xs.at[t, pl.ds((s + 1) * TD + start, rows.size), cols],
+            send_sem=zsend.at[q, s, d],
+            recv_sem=zrecv.at[q, s, d],
             device_id=ring[d],
             device_id_type=MESH,
         )
 
-    def pass_on(t, s):
-        for q in range(2):
+    def pass_on(pieces, s):
+        for q in pieces:
             for d in range(2):
-                hop(t, s - 1, d, q).wait_recv()
+                hop(q, s - 1, d).wait_recv()
 
                 @pl.when(s < NB - 1)
                 def _():
-                    hop(t, s, d, q).start()
+                    hop(q, s, d).start()
 
     def rs_copy(t, s, k):
         p = col_partner(k)
@@ -155,12 +166,17 @@
         total = part[t, s, pl.ds(c * RC, RC)].astype(F32)
         for k in range(NC - 1):
             total += share[t, s, k].astype(F32)
-        if t == 0:
+        rows = pl.ds(s * TD + c * RC, RC)
+
+        @pl.when(t == 0)
+        def _():
             pre[s] = total
-            value = gelu(total)
-        else:
-            value = total * gelu_grad(pre[s])
-        act[t, pl.ds(s * TD + c * RC, RC)] = value.astype(BF16)
+            act[0, rows] = gelu(total).astype(BF16)
+
+        @pl.when(t == 1)
+        def _():
+            act[1, rows] = (total * gelu_grad(pre[s])).astype(BF16)
+
         for k in range(1, NC):
             ag_copy(t, s, k).start()
 
@@ -168,70 +184,6 @@
         wait_bytes(ag_recv.at[t, s], act.at[t, pl.ds(s * TD, (NC - 1) * RC)])
         cols = pl.ds(pl.multiple_of(s * TD, TD), TD)
         act_t[t, :, cols] = act[t, pl.ds(s * TD, TD)].T
-
-    loads[0].wait()
-    for q in range(2):
-        for d in range(2):
-            hop(0, 0, d, q).start()
-        if q == 0:
-            for d in range(2):
-                hop(0, 0, d, q).wait_send()
-    loads[1].wait()
-    loads[2].wait()
-
-    def tokens_step(s, carry):
-        @pl.when(s > 0)
-        def _():
-            pass_on(0, s)
-
-        @pl.when(s == NB - 2)
-        def _():
-            for q in range(2):
-                for d in range(2):
-                    hop(1, 0, d, q).start()
-
-        multiply(0, s)
-
-        @pl.when(s > 0)
-        def _():
-            reduce(0, s - 1)
-
-        @pl.when(s > 1)
-        def _():
-            arrived(0, s - 2)
-
-        return carry
-
-    lax.fori_loop(0, NB, tokens_step, 0)
-    loads[3].wait()
-
-    def grads_step(s, carry):
-        @pl.when(s > 0)
-        def _():
-            pass_on(1, s)
-
-        multiply(1, s)
-
-        @pl.when(s == 0)
-        def _():
-            reduce(0, NB - 1)
-            arrived(0, NB - 2)
-
-        @pl.when(s == 1)
-        def _():
-            arrived(0, NB - 1)
-
-        @pl.when(s > 0)
-        def _():
-            reduce(1, s - 1)
-
-        @pl.when(s > 1)
-        def _():
-            arrived(1, s - 2)
-
-        return carry
-
-    lax.fori_loop(0, NB, grads_step, 0)
 
     def remote(src, dst, sems, device):
         return pltpu.make_async_remote_copy(
@@ -252,7 +204,7 @@
         return remote(ys.at[n, j], yr.at[n, j], ysem.at[n, j, 1], partner)
 
     def tile_cols(j, k):
-        return pl.ds(pl.multiple_of(k * DH + j * TC, 128), TC)
+        return pl.ds(pl.multiple_of(j * CW + k * TC, 128), TC)
 
     def fin_copy(n, j):
         ref = fin[n].at[:, tile_cols(j, core)]
@@ -261,10 +213,16 @@
     def block(n, j, k):
         return dot_nn(act_t[n], xs[1 - n, :, tile_cols(j, k)]) * scale
 
-    def y_start(n, j):
+    def y_give(n, j):
         ss[n, j] = block(n, j, 1 - core).astype(BF16)
         core_copy(n, j).start()
+
+    def y_keep(n, j):
         own[n, j] = block(n, j, core)
+
+    def y_start(n, j):
+        y_give(n, j)
+        y_keep(n, j)
 
     def y_middle(n, j):
         core_copy(n, j).wait_recv()
@@ -286,6 +244,51 @@
             @pl.when((j >= n * YJ) & (j < (n + 1) * YJ))
             def _():
                 step(n, j - n * YJ)
+
+    loads[0].wait()
+    for d in range(2):
+        hop(0, 0, d).start()
+    for d in range(2):
+        hop(0, 0, d).wait_send()
+    for d in range(2):
+        hop(1, 0, d).start()
+    loads[2].wait()
+    loads[1].wait()
+
+    def gather_step(u, carry):
+        t, s = u // NB, u % NB
+        def pass_pieces(part_of):
+            for n, pieces in enumerate((FIRST, SECOND)):
+
+                @pl.when((t == n) & (s > 0))
+                def _():
+                    pass_on(part_of(pieces), s)
+
+        pass_pieces(lambda pieces: pieces[:1])
+        @pl.when(u == NB)
+        def _():
+            loads[3].wait()
+
+        @pl.when(u >= LAG_SUM)
+        def _():
+            reduce((u - LAG_SUM) // NB, (u - LAG_SUM) % NB)
+
+        @pl.when(u >= LAG_ACT)
+        def _():
+            arrived((u - LAG_ACT) // NB, (u - LAG_ACT) % NB)
+
+        pass_pieces(lambda pieces: pieces[1:])
+
+        @pl.when(u == NB - 2)
+        def _():
+            for q in SECOND:
+                for d in range(2):
+                    hop(q, 0, d).start()
+
+        multiply(t, s)
+        return carry
+
+    lax.fori_loop(0, 2 * NB, gather_step, 0)
 
     def z_copy(k, h, d):
         rows = pl.ds(d * HALF, HALF)
@@ -325,9 +328,15 @@
             gt_out[:, pl.ds(pl.multiple_of(h * DH, 128), DH)] = (value + zrb[k - 1, h].astype(F32)).astype(BF16)
 
     def slot(g, carry):
+        @pl.when(g == 0)
+        def _():
+            reduce(1, NB - 2)
+            arrived(1, NB - 4)
+
         @pl.when(g == 1)
         def _():
             reduce(1, NB - 1)
+            arrived(1, NB - 3)
 
         @pl.when(g == 2)
         def _():
@@ -340,24 +349,24 @@
         def _():
             z_slot(i)
 
-        j = g // 3
-
-        @pl.when(g % 3 == 0)
+        j = g // 2
+
+        @pl.when(g % 2 == 0)
         def _():
             at_tile(y_start, j)
 
-        @pl.when(g % 3 == 1)
+        @pl.when(g % 2 == 1)
         def _():
             at_tile(y_middle, j)
 
-        @pl.when(g % 3 == 2)
-        def _():
-            at_tile(y_final, j - 1)
-            at_tile(y_end, j - 2)
+        @pl.when((g % 2 == 0) & (g >= LATE))
+        def _():
+            at_tile(y_final, (g - LATE) // 2)
+            at_tile(y_end, (g - LATE) // 2 - 1)
 
         return carry
 
-    lax.fori_loop(0, 3 * (2 * YJ + 2), slot, 0)
+    lax.fori_loop(0, LATE + 2 * (2 * YJ + 1), slot, 0)
 
 
     def drain_tiles(j, carry):
@@ -371,16 +380,16 @@
 
     def drain_hops(s, carry):
         for d in range(2):
-            for q in range(2):
-                for t in range(2):
-                    if t == 0 and q == 0:
-
-                        @pl.when(s > 0)
-                        def _():
-                            hop(t, s, d, q).wait_send()
-                    else:
-                        hop(t, s, d, q).wait_send()
-                z_copy(s, q, d).wait_send()
+            for q in range(len(PIECES)):
+                if q == 0:
+
+                    @pl.when(s > 0)
+                    def _():
+                        hop(q, s, d).wait_send()
+                else:
+                    hop(q, s, d).wait_send()
+            for h in range(2):
+                z_copy(s, h, d).wait_send()
         return carry
 
     lax.fori_loop(0, NB - 1, drain_hops, 0)
@@ -392,6 +401,21 @@
         return carry
 
     lax.fori_loop(0, NB, drain_sums, 0)
+
+
+def move_out(*refs):
+    *pairs, sem = refs
+    copies = []
+    for n in range(3):
+        src, dst = pairs[n], pairs[3 + n]
+        rows = src.shape[0] // 2
+        for h in range(2):
+            part = pl.ds(h * rows, rows)
+            copies.append(pltpu.make_async_copy(src.at[part], dst.at[part], sem.at[n, h]))
+    for copy in copies:
+        copy.start()
+    for copy in copies:
+        copy.wait()
 
 
 def shards(tokens, grad_out, w_in, w_out):
@@ -426,8 +450,8 @@
             pltpu.VMEM((2, YJ, FL, TC), BF16),
             pltpu.VMEM((2, YJ, FL, TC), BF16),
             dma((4,)),
-            dma((2, NB - 1, 2, 2)),
-            dma((2, NB - 1, 2, 2)),
+            dma((len(PIECES), NB - 1, 2)),
+            dma((len(PIECES), NB - 1, 2)),
             dma((2, NB)),
             dma((2, NB)),
             dma((2, NB)),
@@ -443,6 +467,18 @@
             flops=flops, bytes_accessed=16 * 2**20, transcendentals=4 * rows * FL // NC
         ),
     )(tokens, grad_out, w_in.T, w_out)
+    grad_tokens, grad_in_t, grad_outw = pl.pallas_call(
+        move_out,
+        out_shape=(
+            jax.ShapeDtypeStruct((TD, DL), BF16),
+            jax.ShapeDtypeStruct((FL, DL), BF16),
+            jax.ShapeDtypeStruct((FL, DL), BF16),
+        ),
+        in_specs=[pl.BlockSpec(memory_space=pltpu.VMEM)] * 3,
+        out_specs=(any_space,) * 3,
+        scratch_shapes=[dma((3, 2))],
+        compiler_params=pltpu.CompilerParams(vmem_limit_bytes=8 * 2**20),
+    )(grad_tokens, grad_in_t, grad_outw)
     return grad_tokens, grad_in_t.T, grad_outw
 
 

time: 177 us -> 175 us (0.989)
  local copies, waits for them, and re-layouts: 3.82 us -> 0 us
  Pallas kernels: 172 us -> 174 us
    unnamed x3 -> x0, local copies, waits for them, and re-layouts: 3.82 us -> none
    pallas_call x0 -> x1, Pallas kernels: none -> 2.62 us  [shards(): pl.pallas_call(move_out, out_shape=(jax.ShapeDtypeStruct((TD, DL), BF16),...]
where the time goes in v3:
time: 175 us
  Pallas kernels  174 us (99%)
    pallas_call x1, Pallas kernels, shards(): pl.pallas_call(functools.partial(kernel, scale), out_shape=(pltpu.VMEM((T...  171 us

profile of v3, /device:TPU:1, one launch (start us, length us, event | category | flops | bytes accessed | tf_op | source)
XLA Modules:
  0.0 174.5 jit_solution(16974710196096970612)
XLA Ops:
  0.6 171.3 %shard_map.67 = (bf16[128,2304]{1,0:T(8,128)(2,1)S(1)}, bf16[576,2304]{1,0:T(8,128)(2,1)S(1)}, bf16[576,2304]{1,0:T(8,128)(2,1)S(1)}) custom-call(bf16[128,2304]{1,0:T(8,128)(2,1)} %tokens.1, bf16[128,2304]{1,0:T(8,128)(2,1)} %grad_out.1, bf16[576,2304]{1,0:T(8,128)(2,1)} %bitcast.2, bf16[576,2304]{1,0:T(8,128)(2,1)} %w_out.1), custom_call_target="tpu_custom_call" | custom-call | flops 13589544960 | bytes 16777216 | tf_op jit(solution)/shard_map/pallas_call | solution.py:428
  171.9 2.6 %shard_map.68 = (bf16[128,2304]{1,0:T(8,128)(2,1)}, bf16[576,2304]{1,0:T(8,128)(2,1)}, bf16[576,2304]{1,0:T(8,128)(2,1)}) custom-call(bf16[128,2304]{1,0:T(8,128)(2,1)S(1)} %get-tuple-element.9.refs_0_, bf16[576,2304]{1,0:T(8,128)(2,1)S(1)} %get-tuple-element.10.refs_1_, bf16[576,2304]{1,0:T(8,128)(2,1)S(1)} %get-tuple-element.11.refs_2_), custom_call_target="tpu_custom_call" | custom-call | tf_op jit(solution)/shard_map/pallas_call | solution.py:470

commit v4 on v3

--- a/solution.py
+++ b/solution.py
@@ -99,8 +99,7 @@
         pltpu.make_async_copy(grad_out, xs.at[1, pl.ds(0, TD)], load_sem.at[2]),
         pltpu.make_async_copy(w_out, w.at[1], load_sem.at[3]),
     ]
-    for copy in loads:
-        copy.start()
+    loads[0].start()
 
     barrier = pltpu.get_barrier_semaphore()
     peers = list(ring) + [sibling, partner]
@@ -248,6 +247,8 @@
     loads[0].wait()
     for d in range(2):
         hop(0, 0, d).start()
+    for copy in loads[1:]:
+        copy.start()
     for d in range(2):
         hop(0, 0, d).wait_send()
     for d in range(2):

time: 175 us -> 175 us (level)
  no operation moved by 1% of the time
where the time goes in v4:
time: 175 us
  Pallas kernels  174 us (99%)
    pallas_call x1, Pallas kernels, shards(): pl.pallas_call(functools.partial(kernel, scale), out_shape=(pltpu.VMEM((T...  171 us

profile of v4, /device:TPU:1, one launch (start us, length us, event | category | flops | bytes accessed | tf_op | source)
XLA Modules:
  0.0 174.5 jit_solution(12480469152917733864)
XLA Ops:
  0.6 171.3 %shard_map.67 = (bf16[128,2304]{1,0:T(8,128)(2,1)S(1)}, bf16[576,2304]{1,0:T(8,128)(2,1)S(1)}, bf16[576,2304]{1,0:T(8,128)(2,1)S(1)}) custom-call(bf16[128,2304]{1,0:T(8,128)(2,1)} %tokens.1, bf16[128,2304]{1,0:T(8,128)(2,1)} %grad_out.1, bf16[576,2304]{1,0:T(8,128)(2,1)} %bitcast.2, bf16[576,2304]{1,0:T(8,128)(2,1)} %w_out.1), custom_call_target="tpu_custom_call" | custom-call | flops 13589544960 | bytes 16777216 | tf_op jit(solution)/shard_map/pallas_call | solution.py:429
  171.9 2.6 %shard_map.68 = (bf16[128,2304]{1,0:T(8,128)(2,1)}, bf16[576,2304]{1,0:T(8,128)(2,1)}, bf16[576,2304]{1,0:T(8,128)(2,1)}) custom-call(bf16[128,2304]{1,0:T(8,128)(2,1)S(1)} %get-tuple-element.9.refs_0_, bf16[576,2304]{1,0:T(8,128)(2,1)S(1)} %get-tuple-element.10.refs_1_, bf16[576,2304]{1,0:T(8,128)(2,1)S(1)} %get-tuple-element.11.refs_2_), custom_call_target="tpu_custom_call" | custom-call | tf_op jit(solution)/shard_map/pallas_call | solution.py:471
